TPU v7x, 32 devices: a whole 2x2x4 slice. The times are simulated.
32 devices in a mesh: rep: 2 (over y), tp: 4 (over z), ad: 2 (over x), sub: 2 (over core).
Axes of the slice: x: 2, y: 2, z: 4, core: 2. Of those that a mesh axis runs over, the one named last changes fastest.
Arguments:
- tokens: bfloat16 [4, 512, 8192], P(('rep', 'ad'), None, 'tp'), parts along dimension 0, may hold values from -6 to 6
- query_weight_matrix: bfloat16 [8192, 4096], P('tp', 'sub'), may hold values from -0.0625 to 0.0625
- adapter_down_weight: bfloat16 [24, 16, 8192], P('ad', None, 'tp'), may hold values from -0.0625 to 0.0625
- adapter_up_weight: bfloat16 [24, 16, 4096], P('ad', None, 'sub'), may hold values from -0.75 to 0.75
- request_adapter_id: int32 [4, 8], P('rep'), parts along dimension 0, may hold values from 0 to 23, as said below
- request_token_length: int32 [4, 8], P(('rep', 'ad')), parts along dimension 0, may hold values from 1 to 256, 512 in all within a row
- adapter_store_slot: int32 [48], P('rep'), parts along dimension 0, may hold values from 0 to 23, as said below
Outputs:
- query: bfloat16 [4, 512, 4096], P(('rep', 'ad'), 'tp', 'sub'), parts along dimension 0
There are 2 independent parts, one for each index of `rep`. A program takes and returns all parts, laid end to end along the dimension named above; an argument that names none is the same for every part. Nothing has to cross between parts.
Inputs may be any that keep to these rules, and one draw needn't show every extreme that they name: `request_adapter_id`: among the 8 requests of one group, at most 4 use adapters whose slot lies on one index of ad (slot // 12); in every group exactly 4 use one such index, a different one from group to group. A permutation: adapter a is row adapter_store_slot[a] of the store, held by index adapter_store_slot[a] // 12 of ad.
All inputs are finite; a program needn't handle non-finite values.
Results may differ from a plain program's by a relative error of at most 0.013.
Values may be sent and summed in bfloat16 or wider, within the bound.
A program may use at most 64 MiB of HBM per device.

v0:
```python
import jax
import jax.numpy as jnp
from jax import lax
from jax.sharding import PartitionSpec as P

CAP = 4


ADAPTER_SCALE = 2.0


def local(
    tokens,
    query_weight_matrix,
    adapter_down_weight,
    adapter_up_weight,
    request_adapter_id,
    request_token_length,
    adapter_store_slot,
):
    group_index = lax.axis_index("ad")
    tp_count = lax.axis_size("tp")
    tp_index = lax.axis_index("tp")
    local_rows = tokens[0]
    tok_rows, width_part = local_rows.shape
    half_cols = query_weight_matrix.shape[1]
    store_row_block = adapter_down_weight.shape[0]
    rank_extent = adapter_down_weight.shape[1]
    groups, requests = request_adapter_id.shape
    n_adapters = adapter_store_slot.shape[0]
    own_rows = tok_rows // tp_count
    matches = (
        request_adapter_id[:, :, None] == jnp.arange(n_adapters, dtype=jnp.int32)[None, None, :]
    )
    request_store_slot = jnp.sum(jnp.where(matches, adapter_store_slot[None, None, :], 0), axis=2)
    owners = request_store_slot // store_row_block
    within = request_store_slot % store_row_block
    same_owner = owners[:, :, None] == owners[:, None, :]
    earlier = jnp.arange(requests)[None, :] < jnp.arange(requests)[:, None]
    owner_rank = jnp.sum(jnp.where(same_owner & earlier[None, :, :], 1, 0), axis=2)
    owned = (owners == group_index).astype(jnp.float32)
    rank_hot = (owner_rank[:, :, None] == jnp.arange(CAP)[None, None, :]).astype(jnp.float32)
    slot_hot = (within[:, :, None] == jnp.arange(store_row_block)[None, None, :]).astype(
        jnp.float32
    )
    adapter_selector = jnp.einsum("grc,gra->gca", owned[:, :, None] * rank_hot, slot_hot)
    adapter_selector = adapter_selector.reshape(groups * CAP, store_row_block).astype(jnp.bfloat16)
    send_down = jnp.dot(
        adapter_selector,
        adapter_down_weight.reshape(store_row_block, -1),
        preferred_element_type=jnp.float32,
    )
    send_down = send_down.astype(jnp.bfloat16).reshape(groups, CAP, -1)
    own_owner = lax.dynamic_index_in_dim(owners, group_index, 0, keepdims=False)
    own_rank = lax.dynamic_index_in_dim(owner_rank, group_index, 0, keepdims=False)
    picker = (own_owner[:, None, None] == jnp.arange(groups)[None, :, None]) & (
        own_rank[:, None, None] == jnp.arange(CAP)[None, None, :]
    )
    picker = picker.astype(jnp.bfloat16).reshape(requests, groups * CAP)
    lengths = request_token_length[0]
    seg_ends = jnp.cumsum(lengths)
    seg_starts = seg_ends - lengths
    positions = jnp.arange(tok_rows, dtype=jnp.int32)
    token_mask = (
        (positions[:, None] >= seg_starts[None, :]) & (positions[:, None] < seg_ends[None, :])
    ).astype(jnp.float32)
    forward_up_weight = jnp.dot(
        adapter_selector,
        adapter_up_weight.reshape(store_row_block, -1),
        preferred_element_type=jnp.float32,
    )
    forward_up_weight = forward_up_weight.astype(jnp.bfloat16).reshape(groups, CAP, -1)
    got_down, got_up = (
        lax.all_to_all(send_down, "ad", split_axis=0, concat_axis=0, tiled=True),
        lax.all_to_all(forward_up_weight, "ad", split_axis=0, concat_axis=0, tiled=True),
    )
    request_down_weight = jnp.dot(
        picker, got_down.reshape(groups * CAP, -1), preferred_element_type=jnp.float32
    )
    request_down_weight = request_down_weight.astype(jnp.bfloat16).reshape(
        requests * rank_extent, width_part
    )
    down_acts = jnp.einsum(
        "td,kd->tk", local_rows, request_down_weight, preferred_element_type=jnp.float32
    )
    rank_part = jnp.sum(
        token_mask[:, :, None] * down_acts.reshape(tok_rows, requests, rank_extent), axis=1
    )
    rank_acts = lax.psum(rank_part.astype(jnp.bfloat16), "tp")
    expanded_rows = token_mask[:, :, None] * rank_acts[:, None, :].astype(jnp.float32)
    expanded_rows = expanded_rows.reshape(tok_rows, requests * rank_extent).astype(jnp.bfloat16)
    request_up_weight = jnp.dot(
        picker, got_up.reshape(groups * CAP, -1), preferred_element_type=jnp.float32
    )
    request_up_weight = request_up_weight.astype(jnp.bfloat16).reshape(
        requests * rank_extent, half_cols
    )
    local_token_rows = lax.dynamic_slice_in_dim(expanded_rows, tp_index * own_rows, own_rows, 0)
    adapter_output = jnp.dot(
        local_token_rows, request_up_weight, preferred_element_type=jnp.float32
    )
    base_query_sum = lax.psum_scatter(
        jnp.dot(local_rows, query_weight_matrix, preferred_element_type=jnp.float32).astype(
            jnp.bfloat16
        ),
        "tp",
        scatter_dimension=0,
        tiled=True,
    ).astype(jnp.float32)
    query_output = (base_query_sum + ADAPTER_SCALE * adapter_output).astype(jnp.bfloat16)
    return query_output[None]


def solution(mesh):
    return jax.shard_map(
        local,
        mesh=mesh,
        in_specs=(
            P(("rep", "ad"), None, "tp"),
            P("tp", "sub"),
            P("ad", None, "tp"),
            P("ad", None, "sub"),
            P("rep", None),
            P(("rep", "ad"), None),
            P("rep"),
        ),
        out_specs=P(("rep", "ad"), "tp", "sub"),
        check_vma=False,
    )
```

profile of v0, /device:TPU:0, one launch (start us, length us, event | category | flops | bytes accessed | tf_op | source)
XLA Modules:
  0.0 78.1 jit_solution(16049715495667785892)
XLA Ops:
  6.5 1.6 %copy-done = bf16[1,512,2048]{2,1,0:T(8,128)(2,1)S(1)} copy-done((bf16[1,512,2048]{2,1,0:T(8,128)(2,1)S(1)}, bf16[1,512,2048]{2,1,0:T(8,128)(2,1)}, u32[]{:S(2)}) %copy-start) | copy-done | bytes 2097176
  8.1 9.1 %convolution_convert_fusion.2 = bf16[512,2048]{1,0:T(8,128)(2,1)} fusion(bf16[2048,2048]{1,0:T(8,128)(2,1)} %param.8, bf16[1,512,2048]{2,1,0:T(8,128)(2,1)S(1)} %copy-done), kind=kOutput, calls=%fused_computation.6 | convolution fusion | flops 4296015872 | bytes 12582912 | tf_op jit(solution)/shard_map/dot_general | solution.py:103
  17.3 1.1 %copy-done.2 = bf16[12,16,2048]{2,1,0:T(8,128)(2,1)S(1)} copy-done((bf16[12,16,2048]{2,1,0:T(8,128)(2,1)S(1)}, bf16[12,16,2048]{2,1,0:T(8,128)(2,1)}, u32[]{:S(2)}) %copy-start.2) | copy-done | bytes 786456
  18.4 0.6 copy.9
  19.1 0.2 select_reduce_fusion.1
  19.3 0.2 select_reduce_fusion
  19.5 0.2 convolution_convert_fusion.3
  19.7 0.3 convolution_convert_fusion
  20.0 1.0 %reshape.191 = bf16[2,4,32768]{2,1,0:T(4,128)(2,1)} reshape(bf16[8,32768]{1,0:T(8,128)(2,1)S(1)} %convolution_convert_fusion) | data formatting | bytes 1048576 | tf_op jit(solution)/shard_map/reshape | solution.py:72
  21.0 4.2 %all-to-all-start.1 = ((bf16[2,4,32768]{2,1,0:T(4,128)(2,1)}), bf16[2,4,32768]{2,1,0:T(4,128)(2,1)}, u32[]{:S(2)}, u32[]{:S(2)}) async-start(bf16[2,4,32768]{2,1,0:T(4,128)(2,1)} %reshape.191), calls=%async_computation.2 | async-start | bytes 1048576 | tf_op jit(solution)/shard_map/all_to_all | solution.py:75
  25.4 0.6 copy.8
  26.0 0.2 reduce-window.4
  26.1 1.1 %convolution_convert_fusion.1 = bf16[8,32768]{1,0:T(8,128)(2,1)} fusion(bf16[8,12]{1,0:T(8,128)(2,1)S(1)} %bitcast.54, bf16[12,32768]{1,0:T(8,128)(2,1)S(1)} %bitcast.48), kind=kOutput, calls=%fused_computation.5 | convolution fusion | flops 6553600 | bytes 1310912 | tf_op jit(solution)/shard_map/dot_general | solution.py:48
  27.3 2.0 %reshape.187 = bf16[2,4,32768]{2,1,0:T(4,128)(2,1)} reshape(bf16[8,32768]{1,0:T(8,128)(2,1)} %convolution_convert_fusion.1) | data formatting | bytes 1048576 | tf_op jit(solution)/shard_map/reshape | solution.py:53
  29.4 5.4 %all-to-all-done.1 = bf16[2,4,32768]{2,1,0:T(4,128)(2,1)} async-done(((bf16[2,4,32768]{2,1,0:T(4,128)(2,1)}), bf16[2,4,32768]{2,1,0:T(4,128)(2,1)}, u32[]{:S(2)}, u32[]{:S(2)}) %all-to-all-start.1) | async-done | bytes 524320 | tf_op jit(solution)/shard_map/all_to_all | solution.py:75
  34.8 3.5 %all-to-all-start = ((bf16[2,4,32768]{2,1,0:T(4,128)(2,1)}), bf16[2,4,32768]{2,1,0:T(4,128)(2,1)S(1)}, u32[]{:S(2)}, u32[]{:S(2)}) async-start(bf16[2,4,32768]{2,1,0:T(4,128)(2,1)} %reshape.187), calls=%async_computation.1 | async-start | bytes 1048576 | tf_op jit(solution)/shard_map/all_to_all | solution.py:74
  38.3 1.5 %fusion.1 = bf16[8,32768]{1,0:T(8,128)(2,1)S(1)} fusion(bf16[2,4,32768]{2,1,0:T(4,128)(2,1)} %all-to-all-done.1, pred[8,4]{0,1:T(4,128)(4,1)S(1)} %iota_compare_fusion.8, pred[8,2]{0,1:T(4,128)(4,1)S(1)} %iota_compare_fusion.9), kind=kOutput, calls=%fused_computation.3 | convolution fusion | flops 4456512 | bytes 1048624 | tf_op jit(solution)/shard_map/dot_general | solution.py:92
  39.8 1.0 %reshape.192 = bf16[128,2048]{1,0:T(8,128)(2,1)} reshape(bf16[8,32768]{1,0:T(8,128)(2,1)S(1)} %fusion.1) | data formatting | bytes 1048576 | tf_op jit(solution)/shard_map/reshape | solution.py:95
  40.9 5.1 %all-to-all-done = bf16[2,4,32768]{2,1,0:T(4,128)(2,1)S(1)} async-done(((bf16[2,4,32768]{2,1,0:T(4,128)(2,1)}), bf16[2,4,32768]{2,1,0:T(4,128)(2,1)S(1)}, u32[]{:S(2)}, u32[]{:S(2)}) %all-to-all-start) | async-done | bytes 524320 | tf_op jit(solution)/shard_map/all_to_all | solution.py:74
  46.0 0.5 fusion
  46.5 1.1 %reshape.188 = bf16[128,2048]{1,0:T(8,128)(2,1)} reshape(bf16[8,32768]{1,0:T(8,128)(2,1)S(1)} %fusion) | data formatting | bytes 1048576 | tf_op jit(solution)/shard_map/reshape | solution.py:80
  47.5 1.9 %fusion.5 = f32[128,512]{1,0:T(8,128)S(1)} fusion(bf16[128,2048]{1,0:T(8,128)(2,1)} %reshape.188, bf16[1,512,2048]{2,1,0:T(8,128)(2,1)S(1)} %copy-done), kind=kOutput, calls=%fused_computation.11 | convolution fusion | flops 268435456 | bytes 2883584 | tf_op jit(solution)/shard_map/td,kd->tk/dot_general | solution.py:83
  49.4 19.6 %psum.7 = bf16[512,16]{0,1:T(8,128)(2,1)S(1)} all-reduce(bf16[512,16]{0,1:T(8,128)(2,1)S(1)} %multiply_reduce_fusion), channel_id=1, replica_groups=mesh['rep'=2,'tp'=4,'ad'=2,'sub'=2] {'tp'}, use_global_device_ids=true, to_apply=%region_5.6 | all-reduce | flops 8192 | bytes 32768 | tf_op jit(solution)/shard_map/psum | solution.py:89
  69.1 2.2 %fusion.4 = bf16[1,128,2048]{2,1,0:T(8,128)(2,1)} fusion(bf16[128,2048]{1,0:T(8,128)(2,1)S(1)} %copy-done.1, bf16[128,2048]{1,0:T(8,128)(2,1)} %reduce-scatter.2.cloned.1.call-done, bf16[512,128]{0,1:T(8,128)(2,1)S(1)} %bitcast.52, s32[]{:T(128)S(6)} %select_n.48), kind=kOutput, calls=%fused_computation.10 | convolution fusion | flops 68157440 | bytes 1605636 | tf_op jit(solution)/shard_map/dot_general | solution.py:99
  (28 shorter events, 0.5 us)
Async XLA Ops:
  6.5 1.6 %copy-start = (bf16[1,512,2048]{2,1,0:T(8,128)(2,1)S(1)}, bf16[1,512,2048]{2,1,0:T(8,128)(2,1)}, u32[]{:S(2)}) copy-start(bf16[1,512,2048]{2,1,0:T(8,128)(2,1)} %param.7) | copy-start | bytes 6291460
  6.5 62.6 %reduce-scatter.2.cloned.1.call-start = ((), (), s32[]{:S(2)}) async-start(), calls=%async_computation.3 | async-start | bytes 2621440 | tf_op jit(solution)/shard_map/reduce_scatter | solution.py:102
  17.2 1.1 %copy-start.2 = (bf16[12,16,2048]{2,1,0:T(8,128)(2,1)S(1)}, bf16[12,16,2048]{2,1,0:T(8,128)(2,1)}, u32[]{:S(2)}) copy-start(bf16[12,16,2048]{2,1,0:T(8,128)(2,1)} %param.10) | copy-start | bytes 2359300
  17.2 1.8 %copy-start.4 = (s32[2,8]{1,0:T(2,128)S(1)}, s32[2,8]{1,0:T(2,128)}, u32[]{:S(2)}) copy-start(s32[2,8]{1,0:T(2,128)} %param.11) | copy-start | bytes 196
  17.3 1.8 %copy-start.5 = (s32[24]{0:T(128)S(1)}, s32[24]{0:T(128)}, u32[]{:S(2)}) copy-start(s32[24]{0:T(128)} %param.13) | copy-start | bytes 292
  19.0 6.2 %copy-start.3 = (bf16[12,16,2048]{2,1,0:T(8,128)(2,1)S(1)}, bf16[12,16,2048]{2,1,0:T(8,128)(2,1)}, u32[]{:S(2)}) copy-start(bf16[12,16,2048]{2,1,0:T(8,128)(2,1)} %param.9) | copy-start | bytes 2359300
  21.0 13.8 %all-to-all-start.1 = ((bf16[2,4,32768]{2,1,0:T(4,128)(2,1)}), bf16[2,4,32768]{2,1,0:T(4,128)(2,1)}, u32[]{:S(2)}, u32[]{:S(2)}) async-start(bf16[2,4,32768]{2,1,0:T(4,128)(2,1)} %reshape.191), calls=%async_computation.2 | async-start | bytes 1048576 | tf_op jit(solution)/shard_map/all_to_all | solution.py:75
  25.2 0.7 copy-start.6
  34.8 11.2 %all-to-all-start = ((bf16[2,4,32768]{2,1,0:T(4,128)(2,1)}), bf16[2,4,32768]{2,1,0:T(4,128)(2,1)S(1)}, u32[]{:S(2)}, u32[]{:S(2)}) async-start(bf16[2,4,32768]{2,1,0:T(4,128)(2,1)} %reshape.187), calls=%async_computation.1 | async-start | bytes 1048576 | tf_op jit(solution)/shard_map/all_to_all | solution.py:74
  46.4 22.7 %copy-start.1 = (bf16[128,2048]{1,0:T(8,128)(2,1)S(1)}, bf16[128,2048]{1,0:T(8,128)(2,1)}, u32[]{:S(2)}) copy-start(bf16[128,2048]{1,0:T(8,128)(2,1)} %reshape.192) | copy-start | bytes 1572868
Sparse Core Ops, SparseCore 0:
  17.4 46.8 reduce-scatter.1
where the time goes:
time: 78.7 us; the launch traced here: 78.1 us
  blocking collectives  19.6 us (25%)
  matrix products  16.7 us (21%)
  between operations  13.6 us (17%)
  waiting for transfers between devices  10.6 us (13%)
  local copies, waits for them, and re-layouts  9.15 us (12%)
  starting transfers between devices  7.7 us (10%)
  other arithmetic  0.79 us (1%)
    psum x1, blocking collectives, local(): rank_acts = lax.psum(rank_part.astype(jnp.bfloat16), 'tp')  19.6 us
    dot_general x1, matrix products, local(): jnp.dot(local_rows, query_weight_matrix, preferred_element_type=jnp.float32)  9.09 us
    all_to_all x1, waiting for transfers between devices, local(): lax.all_to_all(forward_up_weight, 'ad', split_axis=0, concat_axis=0, tile...  5.45 us
    all_to_all x1, waiting for transfers between devices, local(): lax.all_to_all(send_down, 'ad', split_axis=0, concat_axis=0, tiled=True)  5.11 us
    all_to_all x1, starting transfers between devices, local(): lax.all_to_all(forward_up_weight, 'ad', split_axis=0, concat_axis=0, tile...  4.21 us
    unnamed x18, local copies, waits for them, and re-layouts  4.05 us
    all_to_all x1, starting transfers between devices, local(): lax.all_to_all(send_down, 'ad', split_axis=0, concat_axis=0, tiled=True)  3.49 us
    dot_general x1, matrix products, local(): jnp.dot(local_token_rows, request_up_weight, preferred_element_type=jnp.f...  2.17 us
  transfers between devices with their start and end apart: 3, of which 2 were waited for; matrix products, arithmetic and copies ran while one was open for 16% of the time, Pallas kernels for 0%

commit v1 on v0

v1 whole, which is shorter than its diff:
```python
import functools
import jax
import jax.numpy as jnp
from jax import lax
from jax.experimental import pallas as pl
from jax.experimental.pallas import tpu as pltpu
from jax.sharding import PartitionSpec as P

CAP = 4

ADAPTER_SCALE = 2.0

BLOCK_COLS = 256
LAG = 2
DEPTH = 3

MESH = pl.DeviceIdType.MESH
F32 = jnp.float32
BF16 = jnp.bfloat16


def one_hot(condition):
    return jnp.where(condition, 1.0, 0.0).astype(BF16)


def kernel(
    tp_count,
    groups,
    rank_extent,
    tokens_hbm,
    weight_hbm,
    down_hbm,
    up_hbm,
    ids_ref,
    lengths_ref,
    slots_ref,
    out_hbm,
    tok,
    weight,
    down,
    up,
    stage,
    from_left,
    from_right,
    down_send,
    up_send,
    got_down,
    got_up,
    rank_send,
    rank_got,
    expanded,
    total,
    out_stage,
    tok_sem,
    weight_sem,
    store_sem,
    flow_send_sem,
    left_sem,
    right_sem,
    adapter_send_sem,
    adapter_recv_sem,
    rank_send_sem,
    rank_recv_sem,
    out_sem,
):
    z = lax.axis_index("tp")
    ad = lax.axis_index("ad")
    rows = tok.shape[1]
    blocks = weight.shape[0]
    requests = ids_ref.shape[1]
    store_rows = down.shape[0]
    held = store_rows // rank_extent
    cap_rows = CAP * rank_extent
    lanes = groups * cap_rows
    rank_bits = rank_extent.bit_length() - 1
    last = tp_count - 1

    def tok_copy(chunk):
        return pltpu.make_async_copy(
            tokens_hbm.at[pl.ds(chunk * rows, rows), :], tok.at[chunk], tok_sem.at[chunk]
        )

    def weight_copy(block):
        return pltpu.make_async_copy(
            weight_hbm.at[:, pl.ds(pl.multiple_of(block * BLOCK_COLS, BLOCK_COLS), BLOCK_COLS)],
            weight.at[block],
            weight_sem.at[block],
        )

    down_copy = pltpu.make_async_copy(down_hbm, down, store_sem.at[0])
    up_copy = pltpu.make_async_copy(up_hbm, up, store_sem.at[1])
    tok_copy(last).start()
    tok_copy(0).start()
    weight_copy(0).start()
    for chunk in range(1, last):
        tok_copy(chunk).start()
    weight_copy(1).start()
    down_copy.start()
    up_copy.start()
    for block in range(2, blocks):
        weight_copy(block).start()

    barrier = pltpu.get_barrier_semaphore()
    for axis, size in (("tp", tp_count), ("ad", groups)):
        for hop in range(1, size):
            other = lax.rem(lax.axis_index(axis) + hop, size)
            pl.semaphore_signal(barrier, inc=1, device_id={axis: other}, device_id_type=MESH)
    pl.semaphore_wait(barrier, tp_count + groups - 2)

    def right_copy(k):
        return pltpu.make_async_remote_copy(
            stage.at[last * blocks - k + 2 * lax.rem(k, blocks)],
            from_left.at[k],
            flow_send_sem.at[last * blocks - k + 2 * lax.rem(k, blocks)],
            left_sem.at[k],
            device_id={"tp": lax.rem(z + 1, tp_count)},
            device_id_type=MESH,
        )

    def left_copy(k):
        return pltpu.make_async_remote_copy(
            stage.at[k],
            from_right.at[k],
            flow_send_sem.at[k],
            right_sem.at[k],
            device_id={"tp": lax.rem(z + last, tp_count)},
            device_id_type=MESH,
        )

    def base_part(chunk, block):
        part = jnp.dot(tok[chunk], weight[block], preferred_element_type=F32)
        return part.astype(BF16)

    def adapter_copy(which, hop):
        send, got = ((down_send, got_down), (up_send, got_up))[which]
        return pltpu.make_async_remote_copy(
            send.at[hop - 1],
            got.at[ad],
            adapter_send_sem.at[which, hop - 1],
            adapter_recv_sem.at[which, hop - 1],
            device_id={"ad": lax.rem(ad + hop, groups)},
            device_id_type=MESH,
        )

    def rank_copy(hop):
        target = lax.rem(z + hop, tp_count)
        return pltpu.make_async_remote_copy(
            rank_send.at[target],
            rank_got.at[hop - 1],
            rank_send_sem.at[hop - 1],
            rank_recv_sem.at[hop - 1],
            device_id={"tp": target},
            device_id_type=MESH,
        )

    def places(group):
        found = []
        for q in range(requests):
            slot = slots_ref[ids_ref[group, q]]
            owner = jnp.int32(0)
            for g in range(1, groups):
                owner = owner + jnp.where(slot >= g * held, 1, 0)
            rank = jnp.int32(0)
            for earlier, _, _ in found:
                rank = rank + jnp.where(earlier == owner, 1, 0)
            found.append((owner, rank, slot - owner * held))
        return found

    def send_adapters():
        down_copy.wait()
        up_copy.wait()
        row = lax.broadcasted_iota(jnp.int32, (cap_rows, store_rows), 0)
        col = lax.broadcasted_iota(jnp.int32, (cap_rows, store_rows), 1)
        for hop in list(range(1, groups)) + [0]:
            wanted = jnp.full((cap_rows, store_rows), -1 - rank_extent, jnp.int32)
            for owner, rank, within in places(lax.rem(ad + hop, groups)):
                place = jnp.where(owner == ad, rank, -1)
                wanted = jnp.where((row >> rank_bits) == place, within * rank_extent, wanted)
            chosen = one_hot(col == wanted + (row & (rank_extent - 1)))
            for which, (store, send, got) in enumerate(
                ((down, down_send, got_down), (up, up_send, got_up))
            ):
                picked = jnp.dot(chosen, store[...], preferred_element_type=F32).astype(BF16)
                if hop > 0:
                    send[hop - 1] = picked
                    adapter_copy(which, hop).start()
                else:
                    got[ad] = picked

    def token_mask(first, count):
        lane = lax.broadcasted_iota(jnp.int32, (1, lanes), 1) >> rank_bits
        starts = jnp.zeros((1, lanes), jnp.int32)
        ends = jnp.zeros((1, lanes), jnp.int32)
        position = jnp.int32(0)
        for q, (owner, rank, _) in enumerate(places(ad)):
            here = lane == owner * CAP + rank
            starts = jnp.where(here, position, starts)
            position = position + lengths_ref[0, q]
            ends = jnp.where(here, position, ends)
        at = first + lax.broadcasted_iota(jnp.int32, (count, lanes), 0)
        return (at >= starts) & (at < ends)

    def rank_hot():
        lane = lax.broadcasted_iota(jnp.int32, (rank_extent, lanes), 1)
        row = lax.broadcasted_iota(jnp.int32, (rank_extent, lanes), 0)
        return one_hot((lane & (rank_extent - 1)) == row)

    def send_ranks():
        for hop in range(1, groups):
            adapter_copy(0, hop).wait()
        acts = lax.dot_general(
            tok[...].reshape(tp_count * rows, -1),
            got_down[...].reshape(lanes, -1),
            (((1,), (1,)), ((), ())),
            preferred_element_type=F32,
        )
        acts = jnp.where(token_mask(0, tp_count * rows), acts, 0.0).astype(BF16)
        for chunk in range(tp_count):
            rank_send[chunk] = lax.dot_general(
                rank_hot(),
                acts[chunk * rows : (chunk + 1) * rows],
                (((1,), (1,)), ((), ())),
                preferred_element_type=F32,
            ).astype(BF16)
        for hop in range(1, tp_count):
            rank_copy(hop).start()

    def expand_ranks():
        for hop in range(1, tp_count):
            rank_copy(hop).wait()
        for hop in range(1, groups):
            adapter_copy(1, hop).wait()
        rank_acts = rank_send[z].astype(F32)
        for hop in range(1, tp_count):
            rank_acts = rank_acts + rank_got[hop - 1].astype(F32)
        spread = lax.dot_general(
            rank_acts.astype(BF16), rank_hot(), (((0,), (0,)), ((), ())), preferred_element_type=F32
        )
        expanded[...] = jnp.where(token_mask(z * rows, rows), spread, 0.0).astype(BF16)

    def out_copy(block):
        return pltpu.make_async_copy(
            out_stage.at[block],
            out_hbm.at[:, pl.ds(pl.multiple_of(block * BLOCK_COLS, BLOCK_COLS), BLOCK_COLS)],
            out_sem.at[block],
        )

    right_count = (last - z) * blocks
    left_count = z * blocks
    final_step = (tp_count - 2) * blocks + LAG

    def step(s, carry):
        @pl.when(s < blocks)
        def _():
            weight_copy(s).wait()

        @pl.when(s == 0)
        def _():
            tok_copy(last).wait()
            tok_copy(0).wait()

        @pl.when(s == 1)
        def _():
            for chunk in range(1, last):
                tok_copy(chunk).wait()

        k_right = s - LAG * z

        @pl.when((k_right >= DEPTH) & (k_right < right_count + DEPTH))
        def _():
            right_copy(k_right - DEPTH).wait_send()

        @pl.when((k_right >= 0) & (k_right < right_count))
        def _():
            chunk = last - k_right // blocks
            block = lax.rem(k_right, blocks)
            at = chunk * blocks + block
            part = base_part(chunk, block)

            @pl.when(z == 0)
            def _():
                stage[at] = part

            @pl.when(z > 0)
            def _():
                right_copy(k_right).wait_recv()
                stage[at] = (part.astype(F32) + from_left[k_right].astype(F32)).astype(BF16)

            right_copy(k_right).start()

        k_left = s - LAG * (last - z)

        @pl.when((k_left >= DEPTH) & (k_left < left_count + DEPTH))
        def _():
            left_copy(k_left - DEPTH).wait_send()

        @pl.when((k_left >= 0) & (k_left < left_count))
        def _():
            part = base_part(k_left // blocks, lax.rem(k_left, blocks))

            @pl.when(z == last)
            def _():
                stage[k_left] = part

            @pl.when(z < last)
            def _():
                left_copy(k_left).wait_recv()
                stage[k_left] = (part.astype(F32) + from_right[k_left].astype(F32)).astype(BF16)

            left_copy(k_left).start()

        @pl.when(s == 2)
        def _():
            send_adapters()

        @pl.when(s == blocks)
        def _():
            send_ranks()

        @pl.when(s == final_step - 2)
        def _():
            expand_ranks()

        block = s - final_step

        @pl.when((block >= 0) & (block < blocks))
        def _():
            cols = pl.ds(pl.multiple_of(block * BLOCK_COLS, BLOCK_COLS), BLOCK_COLS)
            lora = jnp.dot(
                expanded[...],
                got_up[:, :, cols].reshape(lanes, BLOCK_COLS),
                preferred_element_type=F32,
            )
            total[...] = base_part(z, block).astype(F32) + ADAPTER_SCALE * lora

            @pl.when(z < last)
            def _():
                left_copy(left_count + block).wait_recv()
                total[...] += from_right[left_count + block].astype(F32)

            @pl.when(z > 0)
            def _():
                right_copy(right_count + block).wait_recv()
                total[...] += from_left[right_count + block].astype(F32)

            out_stage[block] = total[...].astype(BF16)
            out_copy(block).start()

        return carry

    lax.fori_loop(0, last * blocks + max(LAG, DEPTH), step, 0)
    for block in range(blocks):
        out_copy(block).wait()


def local(
    tokens,
    query_weight_matrix,
    adapter_down_weight,
    adapter_up_weight,
    request_adapter_id,
    request_token_length,
    adapter_store_slot,
):
    tp_count = lax.axis_size("tp")
    groups = lax.axis_size("ad")
    tok_rows, width = tokens.shape[1:]
    cols = query_weight_matrix.shape[1]
    held, rank_extent = adapter_down_weight.shape[:2]
    rows = tok_rows // tp_count
    blocks = cols // BLOCK_COLS
    cap_rows = CAP * rank_extent
    block = (rows, BLOCK_COLS)
    flow = (tp_count - 1) * blocks
    hbm = pl.BlockSpec(memory_space=pl.ANY)
    smem = pl.BlockSpec(memory_space=pltpu.SMEM)
    dma = pltpu.SemaphoreType.DMA
    query = pl.pallas_call(
        functools.partial(kernel, tp_count, groups, rank_extent),
        out_shape=jax.ShapeDtypeStruct((rows, cols), BF16),
        in_specs=[hbm] * 4 + [smem] * 3,
        out_specs=hbm,
        scratch_shapes=[
            pltpu.VMEM((tp_count, rows, width), BF16),
            pltpu.VMEM((blocks, width, BLOCK_COLS), BF16),
            pltpu.VMEM((held * rank_extent, width), BF16),
            pltpu.VMEM((held * rank_extent, cols), BF16),
            pltpu.VMEM((tp_count * blocks, *block), BF16),
            pltpu.VMEM((flow, *block), BF16),
            pltpu.VMEM((flow, *block), BF16),
            pltpu.VMEM((groups - 1, cap_rows, width), BF16),
            pltpu.VMEM((groups - 1, cap_rows, cols), BF16),
            pltpu.VMEM((groups, cap_rows, width), BF16),
            pltpu.VMEM((groups, cap_rows, cols), BF16),
            pltpu.VMEM((tp_count, rank_extent, rows), BF16),
            pltpu.VMEM((tp_count - 1, rank_extent, rows), BF16),
            pltpu.VMEM((rows, groups * cap_rows), BF16),
            pltpu.VMEM(block, F32),
            pltpu.VMEM((blocks, *block), BF16),
            dma((tp_count,)),
            dma((blocks,)),
            dma((2,)),
            dma((tp_count * blocks,)),
            dma((flow,)),
            dma((flow,)),
            dma((2, groups - 1)),
            dma((2, groups - 1)),
            dma((tp_count - 1,)),
            dma((tp_count - 1,)),
            dma((blocks,)),
        ],
        compiler_params=pltpu.CompilerParams(
            collective_id=0, has_side_effects=True, vmem_limit_bytes=56 * 2**20
        ),
        cost_estimate=pl.CostEstimate(
            flops=2 * tok_rows * width * cols,
            bytes_accessed=2 * width * (cols + tok_rows),
            transcendentals=0,
        ),
        name="query_projection",
    )(
        tokens.reshape(tok_rows, width),
        query_weight_matrix,
        adapter_down_weight.reshape(held * rank_extent, width),
        adapter_up_weight.reshape(held * rank_extent, cols),
        request_adapter_id,
        request_token_length,
        adapter_store_slot,
    )
    return query[None]


def solution(mesh):
    return jax.shard_map(
        local,
        mesh=mesh,
        in_specs=(
            P(("rep", "ad"), None, "tp"),
            P("tp", "sub"),
            P("ad", None, "tp"),
            P("ad", None, "sub"),
            P("rep", None),
            P(("rep", "ad"), None),
            P("rep"),
        ),
        out_specs=P(("rep", "ad"), "tp", "sub"),
        check_vma=False,
    )
```

time: 78.7 us -> 44 us (0.56)
  the two profiles are of different devices: /device:TPU:0 before, /device:TPU:22 now
where the time goes in v1:
time: 44 us; the launch traced here: 43.8 us
  Pallas kernels  41.9 us (95%)
  local copies, waits for them, and re-layouts  1.88 us (4%)
    pallas_call x1, Pallas kernels, local(): pl.pallas_call(functools.partial(kernel, tp_count, groups, rank_extent),...  41.9 us
    unnamed x1, local copies, waits for them, and re-layouts  1.88 us

profile of v1, /device:TPU:22, one launch (start us, length us, event | category | flops | bytes accessed | tf_op | source)
XLA Modules:
  0.0 43.8 jit_solution(18275396744360895665)
XLA Ops:
  0.0 41.9 %query_projection.1 = bf16[128,2048]{1,0:T(8,128)(2,1)} custom-call(bf16[512,2048]{1,0:T(8,128)(2,1)} %bitcast.5, bf16[2048,2048]{1,0:T(8,128)(2,1)} %weight_hbm.1, bf16[192,2048]{1,0:T(8,128)(2,1)} %bitcast.6, bf16[192,2048]{1,0:T(8,128)(2,1)} %bitcast.7, s32[2,8]{1,0:T(2,128)} %ids_ref.1, s32[1,8]{1,0:T(1,128)} %lengths_ref.1, s32[24]{0:T(128)} %slots_ref.1), custom_call_target="tpu_custom_call" | custom-call | flops 4294967296 | bytes 10485760 | tf_op jit(solution)/shard_map/query_projection/pallas_call | solution.py:378
  41.9 1.9 %copy.9 = bf16[1,128,2048]{2,1,0:T(8,128)(2,1)} copy(bf16[1,128,2048]{2,1,0:T(8,128)(2,1)} %bitcast.4) | data formatting | bytes 1048576

commit v2 on v1

--- a/solution.py
+++ b/solution.py
@@ -10,9 +10,9 @@
 
 ADAPTER_SCALE = 2.0
 
-BLOCK_COLS = 256
+BLOCK_COLS = 512
 LAG = 2
-DEPTH = 3
+DEPTH = 4
 
 MESH = pl.DeviceIdType.MESH
 F32 = jnp.float32
@@ -34,7 +34,7 @@
     ids_ref,
     lengths_ref,
     slots_ref,
-    out_hbm,
+    out,
     tok,
     weight,
     down,
@@ -46,11 +46,12 @@
     up_send,
     got_down,
     got_up,
+    rank_own,
     rank_send,
     rank_got,
+    rank_sum,
     expanded,
     total,
-    out_stage,
     tok_sem,
     weight_sem,
     store_sem,
@@ -61,7 +62,6 @@
     adapter_recv_sem,
     rank_send_sem,
     rank_recv_sem,
-    out_sem,
 ):
     z = lax.axis_index("tp")
     ad = lax.axis_index("ad")
@@ -89,23 +89,33 @@
 
     down_copy = pltpu.make_async_copy(down_hbm, down, store_sem.at[0])
     up_copy = pltpu.make_async_copy(up_hbm, up, store_sem.at[1])
-    tok_copy(last).start()
-    tok_copy(0).start()
+    barrier = pltpu.get_barrier_semaphore()
+
+    def greet(target):
+        pl.semaphore_signal(barrier, inc=1, device_id=target, device_id_type=MESH)
+
+    @pl.when(z < last)
+    def _():
+        greet({"tp": lax.rem(z + 1, tp_count)})
+
+    @pl.when(z > 0)
+    def _():
+        greet({"tp": lax.rem(z + last, tp_count)})
+
+    for hop in range(1, groups):
+        greet({"ad": lax.rem(ad + hop, groups)})
+
+    first = jnp.where(z == last, 0, last)
+    tok_copy(first).start()
     weight_copy(0).start()
+    weight_copy(1).start()
+    tok_copy(last - first).start()
     for chunk in range(1, last):
         tok_copy(chunk).start()
-    weight_copy(1).start()
     down_copy.start()
     up_copy.start()
     for block in range(2, blocks):
         weight_copy(block).start()
-
-    barrier = pltpu.get_barrier_semaphore()
-    for axis, size in (("tp", tp_count), ("ad", groups)):
-        for hop in range(1, size):
-            other = lax.rem(lax.axis_index(axis) + hop, size)
-            pl.semaphore_signal(barrier, inc=1, device_id={axis: other}, device_id_type=MESH)
-    pl.semaphore_wait(barrier, tp_count + groups - 2)
 
     def right_copy(k):
         return pltpu.make_async_remote_copy(
@@ -142,14 +152,13 @@
             device_id_type=MESH,
         )
 
-    def rank_copy(hop):
-        target = lax.rem(z + hop, tp_count)
+    def rank_copy(way):
         return pltpu.make_async_remote_copy(
-            rank_send.at[target],
-            rank_got.at[hop - 1],
-            rank_send_sem.at[hop - 1],
-            rank_recv_sem.at[hop - 1],
-            device_id={"tp": target},
+            rank_send.at[way],
+            rank_got.at[way],
+            rank_send_sem.at[way],
+            rank_recv_sem.at[way],
+            device_id={"tp": lax.rem(z + (1 if way == 0 else last), tp_count)},
             device_id_type=MESH,
         )
 
@@ -216,51 +225,78 @@
         )
         acts = jnp.where(token_mask(0, tp_count * rows), acts, 0.0).astype(BF16)
         for chunk in range(tp_count):
-            rank_send[chunk] = lax.dot_general(
+            rank_own[chunk] = lax.dot_general(
                 rank_hot(),
                 acts[chunk * rows : (chunk + 1) * rows],
                 (((1,), (1,)), ((), ())),
                 preferred_element_type=F32,
             ).astype(BF16)
-        for hop in range(1, tp_count):
-            rank_copy(hop).start()
+
+    def pass_ranks(way):
+        @pl.when(z == (0 if way == 0 else last))
+        def _():
+            rank_send[way] = rank_own[...]
+
+        @pl.when(z != (0 if way == 0 else last))
+        def _():
+            rank_copy(way).wait_recv()
+            rank_send[way] = (rank_own[...].astype(F32) + rank_got[way].astype(F32)).astype(BF16)
+
+        rank_copy(way).start()
 
     def expand_ranks():
-        for hop in range(1, tp_count):
-            rank_copy(hop).wait()
         for hop in range(1, groups):
             adapter_copy(1, hop).wait()
-        rank_acts = rank_send[z].astype(F32)
-        for hop in range(1, tp_count):
-            rank_acts = rank_acts + rank_got[hop - 1].astype(F32)
+        rank_sum[...] = rank_own[z].astype(F32)
+
+        @pl.when(z == last)
+        def _():
+            rank_copy(0).wait_recv()
+
+        @pl.when(z > 0)
+        def _():
+            rank_sum[...] += rank_got[0, z].astype(F32)
+
+        @pl.when(z == 0)
+        def _():
+            rank_copy(1).wait_recv()
+
+        @pl.when(z < last)
+        def _():
+            rank_sum[...] += rank_got[1, z].astype(F32)
+
         spread = lax.dot_general(
-            rank_acts.astype(BF16), rank_hot(), (((0,), (0,)), ((), ())), preferred_element_type=F32
+            rank_sum[...].astype(BF16),
+            rank_hot(),
+            (((0,), (0,)), ((), ())),
+            preferred_element_type=F32,
         )
         expanded[...] = jnp.where(token_mask(z * rows, rows), spread, 0.0).astype(BF16)
-
-    def out_copy(block):
-        return pltpu.make_async_copy(
-            out_stage.at[block],
-            out_hbm.at[:, pl.ds(pl.multiple_of(block * BLOCK_COLS, BLOCK_COLS), BLOCK_COLS)],
-            out_sem.at[block],
-        )
 
     right_count = (last - z) * blocks
     left_count = z * blocks
     final_step = (tp_count - 2) * blocks + LAG
 
+    rank_step = blocks + 1
+
+    tok_copy(first).wait()
+    weight_copy(0).wait()
+
+    @pl.when((z == 0) | (z == last))
+    def _():
+        stage[first * blocks] = base_part(first, 0)
+
+    neighbours = jnp.where(z > 0, 1, 0) + jnp.where(z < last, 1, 0)
+    pl.semaphore_wait(barrier, neighbours + groups - 1)
+
     def step(s, carry):
-        @pl.when(s < blocks)
+        @pl.when((s > 0) & (s < blocks))
         def _():
             weight_copy(s).wait()
 
-        @pl.when(s == 0)
-        def _():
-            tok_copy(last).wait()
-            tok_copy(0).wait()
-
         @pl.when(s == 1)
         def _():
+            tok_copy(last - first).wait()
             for chunk in range(1, last):
                 tok_copy(chunk).wait()
 
@@ -275,14 +311,14 @@
             chunk = last - k_right // blocks
             block = lax.rem(k_right, blocks)
             at = chunk * blocks + block
-            part = base_part(chunk, block)
-
-            @pl.when(z == 0)
-            def _():
-                stage[at] = part
+
+            @pl.when((z == 0) & (s > 0))
+            def _():
+                stage[at] = base_part(chunk, block)
 
             @pl.when(z > 0)
             def _():
+                part = base_part(chunk, block)
                 right_copy(k_right).wait_recv()
                 stage[at] = (part.astype(F32) + from_left[k_right].astype(F32)).astype(BF16)
 
@@ -296,28 +332,38 @@
 
         @pl.when((k_left >= 0) & (k_left < left_count))
         def _():
-            part = base_part(k_left // blocks, lax.rem(k_left, blocks))
-
-            @pl.when(z == last)
-            def _():
-                stage[k_left] = part
+            chunk = k_left // blocks
+            block = lax.rem(k_left, blocks)
+
+            @pl.when((z == last) & (s > 0))
+            def _():
+                stage[k_left] = base_part(chunk, block)
 
             @pl.when(z < last)
             def _():
+                part = base_part(chunk, block)
                 left_copy(k_left).wait_recv()
                 stage[k_left] = (part.astype(F32) + from_right[k_left].astype(F32)).astype(BF16)
 
             left_copy(k_left).start()
 
-        @pl.when(s == 2)
+        @pl.when(s == 1)
         def _():
             send_adapters()
 
-        @pl.when(s == blocks)
+        @pl.when(s == rank_step)
         def _():
             send_ranks()
 
-        @pl.when(s == final_step - 2)
+        @pl.when((s == rank_step + z) & (z < last))
+        def _():
+            pass_ranks(0)
+
+        @pl.when((s == rank_step + last - z) & (z > 0))
+        def _():
+            pass_ranks(1)
+
+        @pl.when(s == final_step - 1)
         def _():
             expand_ranks()
 
@@ -343,14 +389,19 @@
                 right_copy(right_count + block).wait_recv()
                 total[...] += from_left[right_count + block].astype(F32)
 
-            out_stage[block] = total[...].astype(BF16)
-            out_copy(block).start()
+            out[:, cols] = total[...].astype(BF16)
 
         return carry
 
     lax.fori_loop(0, last * blocks + max(LAG, DEPTH), step, 0)
-    for block in range(blocks):
-        out_copy(block).wait()
+
+    @pl.when(z < last)
+    def _():
+        rank_copy(0).wait_send()
+
+    @pl.when(z > 0)
+    def _():
+        rank_copy(1).wait_send()
 
 
 def local(
@@ -372,14 +423,14 @@
     cap_rows = CAP * rank_extent
     block = (rows, BLOCK_COLS)
     flow = (tp_count - 1) * blocks
-    hbm = pl.BlockSpec(memory_space=pl.ANY)
+    hbm = pl.BlockSpec(memory_space=pltpu.HBM)
     smem = pl.BlockSpec(memory_space=pltpu.SMEM)
     dma = pltpu.SemaphoreType.DMA
     query = pl.pallas_call(
         functools.partial(kernel, tp_count, groups, rank_extent),
-        out_shape=jax.ShapeDtypeStruct((rows, cols), BF16),
+        out_shape=pltpu.VMEM((rows, cols), BF16),
         in_specs=[hbm] * 4 + [smem] * 3,
-        out_specs=hbm,
+        out_specs=pl.BlockSpec(memory_space=pltpu.VMEM),
         scratch_shapes=[
             pltpu.VMEM((tp_count, rows, width), BF16),
             pltpu.VMEM((blocks, width, BLOCK_COLS), BF16),
@@ -393,10 +444,11 @@
             pltpu.VMEM((groups, cap_rows, width), BF16),
             pltpu.VMEM((groups, cap_rows, cols), BF16),
             pltpu.VMEM((tp_count, rank_extent, rows), BF16),
-            pltpu.VMEM((tp_count - 1, rank_extent, rows), BF16),
+            pltpu.VMEM((2, tp_count, rank_extent, rows), BF16),
+            pltpu.VMEM((2, tp_count, rank_extent, rows), BF16),
+            pltpu.VMEM((rank_extent, rows), F32),
             pltpu.VMEM((rows, groups * cap_rows), BF16),
             pltpu.VMEM(block, F32),
-            pltpu.VMEM((blocks, *block), BF16),
             dma((tp_count,)),
             dma((blocks,)),
             dma((2,)),
@@ -405,9 +457,8 @@
             dma((flow,)),
             dma((2, groups - 1)),
             dma((2, groups - 1)),
-            dma((tp_count - 1,)),
-            dma((tp_count - 1,)),
-            dma((blocks,)),
+            dma((2,)),
+            dma((2,)),
         ],
         compiler_params=pltpu.CompilerParams(
             collective_id=0, has_side_effects=True, vmem_limit_bytes=56 * 2**20

time: 44 us -> 41 us (0.932)
  Pallas kernels: 41.9 us -> 40.1 us
  local copies, waits for them, and re-layouts: 1.88 us -> 0.8 us
    pallas_call x1, Pallas kernels: 41.9 us -> 40.1 us  [local(): pl.pallas_call(functools.partial(kernel, tp_count, groups, rank_extent),...]
    unnamed x1, local copies, waits for them, and re-layouts: 1.88 us -> 0.8 us
where the time goes in v2:
time: 41 us; the launch traced here: 40.9 us
  Pallas kernels  40.1 us (98%)
  local copies, waits for them, and re-layouts  0.8 us (2%)
    pallas_call x1, Pallas kernels, local(): pl.pallas_call(functools.partial(kernel, tp_count, groups, rank_extent),...  40.1 us

profile of v2, /device:TPU:22, one launch (start us, length us, event | category | flops | bytes accessed | tf_op | source)
XLA Modules:
  0.0 40.9 jit_solution(1506359365522601738)
XLA Ops:
  0.0 40.1 %query_projection.1 = bf16[128,2048]{1,0:T(8,128)(2,1)S(1)} custom-call(bf16[512,2048]{1,0:T(8,128)(2,1)} %bitcast.5, bf16[2048,2048]{1,0:T(8,128)(2,1)} %weight_hbm.1, bf16[192,2048]{1,0:T(8,128)(2,1)} %bitcast.6, bf16[192,2048]{1,0:T(8,128)(2,1)} %bitcast.7, s32[2,8]{1,0:T(2,128)} %ids_ref.1, s32[1,8]{1,0:T(1,128)} %lengths_ref.1, s32[24]{0:T(128)} %slots_ref.1), custom_call_target="tpu_custom_call" | custom-call | flops 4294967296 | bytes 10485760 | tf_op jit(solution)/shard_map/query_projection/pallas_call | solution.py:429
  40.1 0.8 %copy.9 = bf16[1,128,2048]{2,1,0:T(8,128)(2,1)} copy(bf16[1,128,2048]{2,1,0:T(8,128)(2,1)S(1)} %bitcast.4) | data formatting | bytes 1048576

commit v3 on v2

--- a/solution.py
+++ b/solution.py
@@ -11,6 +11,7 @@
 ADAPTER_SCALE = 2.0
 
 BLOCK_COLS = 512
+PIECES = ((0, 128), (128, 384))
 LAG = 2
 DEPTH = 4
 
@@ -31,9 +32,9 @@
     weight_hbm,
     down_hbm,
     up_hbm,
-    ids_ref,
-    lengths_ref,
-    slots_ref,
+    ids_hbm,
+    lengths_hbm,
+    slots_hbm,
     out,
     tok,
     weight,
@@ -50,11 +51,14 @@
     rank_send,
     rank_got,
     rank_sum,
-    expanded,
     total,
+    ids_ref,
+    lengths_ref,
+    slots_ref,
     tok_sem,
     weight_sem,
     store_sem,
+    small_sem,
     flow_send_sem,
     left_sem,
     right_sem,
@@ -62,6 +66,9 @@
     adapter_recv_sem,
     rank_send_sem,
     rank_recv_sem,
+    piece_weight_sem,
+    piece_send_sem,
+    piece_recv_sem,
 ):
     z = lax.axis_index("tp")
     ad = lax.axis_index("ad")
@@ -87,8 +94,20 @@
             weight_sem.at[block],
         )
 
+    def first_weight_copy(i):
+        cols = pl.ds(*PIECES[i])
+        return pltpu.make_async_copy(
+            weight_hbm.at[:, cols], weight.at[0, :, cols], piece_weight_sem.at[i]
+        )
+
     down_copy = pltpu.make_async_copy(down_hbm, down, store_sem.at[0])
     up_copy = pltpu.make_async_copy(up_hbm, up, store_sem.at[1])
+    small_copies = [
+        pltpu.make_async_copy(source, target, small_sem.at[i])
+        for i, (source, target) in enumerate(
+            ((ids_hbm, ids_ref), (lengths_hbm, lengths_ref), (slots_hbm, slots_ref))
+        )
+    ]
     barrier = pltpu.get_barrier_semaphore()
 
     def greet(target):
@@ -106,12 +125,16 @@
         greet({"ad": lax.rem(ad + hop, groups)})
 
     first = jnp.where(z == last, 0, last)
+    first_weight_copy(0).start()
     tok_copy(first).start()
-    weight_copy(0).start()
+    for i in range(1, len(PIECES)):
+        first_weight_copy(i).start()
     weight_copy(1).start()
     tok_copy(last - first).start()
     for chunk in range(1, last):
         tok_copy(chunk).start()
+    for small in small_copies:
+        small.start()
     down_copy.start()
     up_copy.start()
     for block in range(2, blocks):
@@ -134,6 +157,18 @@
             flow_send_sem.at[k],
             right_sem.at[k],
             device_id={"tp": lax.rem(z + last, tp_count)},
+            device_id_type=MESH,
+        )
+
+    def piece_copy(way, i):
+        cols = pl.ds(*PIECES[i])
+        got, at, hop = ((from_left, last * blocks, 1), (from_right, 0, last))[way]
+        return pltpu.make_async_remote_copy(
+            stage.at[at, :, cols],
+            got.at[0, :, cols],
+            piece_send_sem.at[way, i],
+            piece_recv_sem.at[way, i],
+            device_id={"tp": lax.rem(z + hop, tp_count)},
             device_id_type=MESH,
         )
 
@@ -176,6 +211,8 @@
         return found
 
     def send_adapters():
+        for small in small_copies:
+            small.wait()
         down_copy.wait()
         up_copy.wait()
         row = lax.broadcasted_iota(jnp.int32, (cap_rows, store_rows), 0)
@@ -271,7 +308,19 @@
             (((0,), (0,)), ((), ())),
             preferred_element_type=F32,
         )
-        expanded[...] = jnp.where(token_mask(z * rows, rows), spread, 0.0).astype(BF16)
+        expanded = jnp.where(token_mask(z * rows, rows), spread, 0.0).astype(BF16)
+
+        def own(block, carry):
+            cols = pl.ds(pl.multiple_of(block * BLOCK_COLS, BLOCK_COLS), BLOCK_COLS)
+            lora = jnp.dot(
+                expanded,
+                got_up[:, :, cols].reshape(lanes, BLOCK_COLS),
+                preferred_element_type=F32,
+            )
+            total[block] = base_part(z, block).astype(F32) + ADAPTER_SCALE * lora
+            return carry
+
+        lax.fori_loop(0, blocks, own, 0)
 
     right_count = (last - z) * blocks
     left_count = z * blocks
@@ -279,15 +328,25 @@
 
     rank_step = blocks + 1
 
+    neighbours = jnp.where(z > 0, 1, 0) + jnp.where(z < last, 1, 0)
     tok_copy(first).wait()
-    weight_copy(0).wait()
-
-    @pl.when((z == 0) | (z == last))
-    def _():
-        stage[first * blocks] = base_part(first, 0)
-
-    neighbours = jnp.where(z > 0, 1, 0) + jnp.where(z < last, 1, 0)
-    pl.semaphore_wait(barrier, neighbours + groups - 1)
+    for i, (low, count) in enumerate(PIECES):
+        cols = pl.ds(low, count)
+        first_weight_copy(i).wait()
+
+        @pl.when((z == 0) | (z == last))
+        def _():
+            part = jnp.dot(tok[first], weight[0, :, cols], preferred_element_type=F32)
+            stage[first * blocks, :, cols] = part.astype(BF16)
+
+        if i == 0:
+            pl.semaphore_wait(barrier, neighbours + groups - 1)
+
+        for way, end in enumerate((0, last)):
+
+            @pl.when(z == end)
+            def _():
+                piece_copy(way, i).start()
 
     def step(s, carry):
         @pl.when((s > 0) & (s < blocks))
@@ -304,7 +363,14 @@
 
         @pl.when((k_right >= DEPTH) & (k_right < right_count + DEPTH))
         def _():
-            right_copy(k_right - DEPTH).wait_send()
+            @pl.when((z == 0) & (k_right == DEPTH))
+            def _():
+                for i in range(len(PIECES)):
+                    piece_copy(0, i).wait_send()
+
+            @pl.when((z != 0) | (k_right > DEPTH))
+            def _():
+                right_copy(k_right - DEPTH).wait_send()
 
         @pl.when((k_right >= 0) & (k_right < right_count))
         def _():
@@ -319,16 +385,34 @@
             @pl.when(z > 0)
             def _():
                 part = base_part(chunk, block)
-                right_copy(k_right).wait_recv()
+
+                @pl.when((z == 1) & (k_right == 0))
+                def _():
+                    for i in range(len(PIECES)):
+                        piece_copy(0, i).wait_recv()
+
+                @pl.when((z != 1) | (k_right > 0))
+                def _():
+                    right_copy(k_right).wait_recv()
+
                 stage[at] = (part.astype(F32) + from_left[k_right].astype(F32)).astype(BF16)
 
-            right_copy(k_right).start()
+            @pl.when((z != 0) | (s > 0))
+            def _():
+                right_copy(k_right).start()
 
         k_left = s - LAG * (last - z)
 
         @pl.when((k_left >= DEPTH) & (k_left < left_count + DEPTH))
         def _():
-            left_copy(k_left - DEPTH).wait_send()
+            @pl.when((z == last) & (k_left == DEPTH))
+            def _():
+                for i in range(len(PIECES)):
+                    piece_copy(1, i).wait_send()
+
+            @pl.when((z != last) | (k_left > DEPTH))
+            def _():
+                left_copy(k_left - DEPTH).wait_send()
 
         @pl.when((k_left >= 0) & (k_left < left_count))
         def _():
@@ -342,10 +426,21 @@
             @pl.when(z < last)
             def _():
                 part = base_part(chunk, block)
-                left_copy(k_left).wait_recv()
+
+                @pl.when((z == last - 1) & (k_left == 0))
+                def _():
+                    for i in range(len(PIECES)):
+                        piece_copy(1, i).wait_recv()
+
+                @pl.when((z != last - 1) | (k_left > 0))
+                def _():
+                    left_copy(k_left).wait_recv()
+
                 stage[k_left] = (part.astype(F32) + from_right[k_left].astype(F32)).astype(BF16)
 
-            left_copy(k_left).start()
+            @pl.when((z != last) | (s > 0))
+            def _():
+                left_copy(k_left).start()
 
         @pl.when(s == 1)
         def _():
@@ -372,24 +467,18 @@
         @pl.when((block >= 0) & (block < blocks))
         def _():
             cols = pl.ds(pl.multiple_of(block * BLOCK_COLS, BLOCK_COLS), BLOCK_COLS)
-            lora = jnp.dot(
-                expanded[...],
-                got_up[:, :, cols].reshape(lanes, BLOCK_COLS),
-                preferred_element_type=F32,
-            )
-            total[...] = base_part(z, block).astype(F32) + ADAPTER_SCALE * lora
 
             @pl.when(z < last)
             def _():
                 left_copy(left_count + block).wait_recv()
-                total[...] += from_right[left_count + block].astype(F32)
+                total[block] += from_right[left_count + block].astype(F32)
 
             @pl.when(z > 0)
             def _():
                 right_copy(right_count + block).wait_recv()
-                total[...] += from_left[right_count + block].astype(F32)
-
-            out[:, cols] = total[...].astype(BF16)
+                total[block] += from_left[right_count + block].astype(F32)
+
+            out[:, cols] = total[block].astype(BF16)
 
         return carry
 
@@ -424,12 +513,11 @@
     block = (rows, BLOCK_COLS)
     flow = (tp_count - 1) * blocks
     hbm = pl.BlockSpec(memory_space=pltpu.HBM)
-    smem = pl.BlockSpec(memory_space=pltpu.SMEM)
     dma = pltpu.SemaphoreType.DMA
     query = pl.pallas_call(
         functools.partial(kernel, tp_count, groups, rank_extent),
         out_shape=pltpu.VMEM((rows, cols), BF16),
-        in_specs=[hbm] * 4 + [smem] * 3,
+        in_specs=[hbm] * 7,
         out_specs=pl.BlockSpec(memory_space=pltpu.VMEM),
         scratch_shapes=[
             pltpu.VMEM((tp_count, rows, width), BF16),
@@ -447,11 +535,14 @@
             pltpu.VMEM((2, tp_count, rank_extent, rows), BF16),
             pltpu.VMEM((2, tp_count, rank_extent, rows), BF16),
             pltpu.VMEM((rank_extent, rows), F32),
-            pltpu.VMEM((rows, groups * cap_rows), BF16),
-            pltpu.VMEM(block, F32),
+            pltpu.VMEM((blocks, *block), F32),
+            pltpu.SMEM(request_adapter_id.shape, jnp.int32),
+            pltpu.SMEM(request_token_length.shape, jnp.int32),
+            pltpu.SMEM(adapter_store_slot.shape, jnp.int32),
             dma((tp_count,)),
             dma((blocks,)),
             dma((2,)),
+            dma((3,)),
             dma((tp_count * blocks,)),
             dma((flow,)),
             dma((flow,)),
@@ -459,6 +550,9 @@
             dma((2, groups - 1)),
             dma((2,)),
             dma((2,)),
+            dma((len(PIECES),)),
+            dma((2, len(PIECES))),
+            dma((2, len(PIECES))),
         ],
         compiler_params=pltpu.CompilerParams(
             collective_id=0, has_side_effects=True, vmem_limit_bytes=56 * 2**20

time: 41 us -> 40 us (0.976)
  Pallas kernels: 40.1 us -> 39.1 us
    pallas_call x1, Pallas kernels: 40.1 us -> 39.1 us  [local(): pl.pallas_call(functools.partial(kernel, tp_count, groups, rank_extent),...]
where the time goes in v3:
time: 40 us; the launch traced here: 39.9 us
  Pallas kernels  39.1 us (98%)
  local copies, waits for them, and re-layouts  0.8 us (2%)
    pallas_call x1, Pallas kernels, local(): pl.pallas_call(functools.partial(kernel, tp_count, groups, rank_extent),...  39.1 us

profile of v3, /device:TPU:22, one launch (start us, length us, event | category | flops | bytes accessed | tf_op | source)
XLA Modules:
  0.0 39.9 jit_solution(17611639747129494849)
XLA Ops:
  0.0 39.1 %query_projection.1 = bf16[128,2048]{1,0:T(8,128)(2,1)S(1)} custom-call(bf16[512,2048]{1,0:T(8,128)(2,1)} %bitcast.5, bf16[2048,2048]{1,0:T(8,128)(2,1)} %weight_hbm.1, bf16[192,2048]{1,0:T(8,128)(2,1)} %bitcast.6, bf16[192,2048]{1,0:T(8,128)(2,1)} %bitcast.7, s32[2,8]{1,0:T(2,128)} %ids_hbm.1, s32[1,8]{1,0:T(1,128)} %lengths_hbm.1, s32[24]{0:T(128)} %slots_hbm.1), custom_call_target="tpu_custom_call" | custom-call | flops 4294967296 | bytes 10485760 | tf_op jit(solution)/shard_map/query_projection/pallas_call | solution.py:517
  39.1 0.8 %copy.9 = bf16[1,128,2048]{2,1,0:T(8,128)(2,1)} copy(bf16[1,128,2048]{2,1,0:T(8,128)(2,1)S(1)} %bitcast.4) | data formatting | bytes 1048576

commit v4 on v3

--- a/solution.py
+++ b/solution.py
@@ -11,9 +11,9 @@
 ADAPTER_SCALE = 2.0
 
 BLOCK_COLS = 512
-PIECES = ((0, 128), (128, 384))
-LAG = 2
-DEPTH = 4
+PIECES = ((0, 128), (128, 128), (256, 256))
+LAG = 3
+DEPTH = 2
 
 MESH = pl.DeviceIdType.MESH
 F32 = jnp.float32
@@ -108,6 +108,10 @@
             ((ids_hbm, ids_ref), (lengths_hbm, lengths_ref), (slots_hbm, slots_ref))
         )
     ]
+    first = jnp.where(z == last, 0, last)
+    first_weight_copy(0).start()
+    tok_copy(first).start()
+
     barrier = pltpu.get_barrier_semaphore()
 
     def greet(target):
@@ -124,9 +128,6 @@
     for hop in range(1, groups):
         greet({"ad": lax.rem(ad + hop, groups)})
 
-    first = jnp.where(z == last, 0, last)
-    first_weight_copy(0).start()
-    tok_copy(first).start()
     for i in range(1, len(PIECES)):
         first_weight_copy(i).start()
     weight_copy(1).start()
@@ -462,23 +463,35 @@
         def _():
             expand_ranks()
 
+        early = s - final_step + 1
+        inner = (early >= 0) & (early < blocks) & (z > 0) & (z < last)
+
+        @pl.when(inner & (2 * z < last))
+        def _():
+            left_copy(left_count + early).wait_recv()
+            total[early] += from_right[left_count + early].astype(F32)
+
+        @pl.when(inner & (2 * z >= last))
+        def _():
+            right_copy(right_count + early).wait_recv()
+            total[early] += from_left[right_count + early].astype(F32)
+
         block = s - final_step
-
-        @pl.when((block >= 0) & (block < blocks))
-        def _():
-            cols = pl.ds(pl.multiple_of(block * BLOCK_COLS, BLOCK_COLS), BLOCK_COLS)
-
-            @pl.when(z < last)
-            def _():
-                left_copy(left_count + block).wait_recv()
-                total[block] += from_right[left_count + block].astype(F32)
-
-            @pl.when(z > 0)
-            def _():
-                right_copy(right_count + block).wait_recv()
-                total[block] += from_left[right_count + block].astype(F32)
-
-            out[:, cols] = total[block].astype(BF16)
+        own = (block >= 0) & (block < blocks)
+        late_left = (z == 0) | ((2 * z >= last) & (z < last))
+        cols = pl.ds(pl.multiple_of(block * BLOCK_COLS, BLOCK_COLS), BLOCK_COLS)
+
+        @pl.when(own & late_left)
+        def _():
+            left_copy(left_count + block).wait_recv()
+            late = from_right[left_count + block].astype(F32)
+            out[:, cols] = (total[block] + late).astype(BF16)
+
+        @pl.when(own & jnp.logical_not(late_left))
+        def _():
+            right_copy(right_count + block).wait_recv()
+            late = from_left[right_count + block].astype(F32)
+            out[:, cols] = (total[block] + late).astype(BF16)
 
         return carry
 

time: 40 us -> 39.5 us (0.988)
  Pallas kernels: 39.1 us -> 38.6 us
    pallas_call x1, Pallas kernels: 39.1 us -> 38.6 us  [local(): pl.pallas_call(functools.partial(kernel, tp_count, groups, rank_extent),...]
where the time goes in v4:
time: 39.5 us; the launch traced here: 39.4 us
  Pallas kernels  38.6 us (98%)
  local copies, waits for them, and re-layouts  0.8 us (2%)
    pallas_call x1, Pallas kernels, local(): pl.pallas_call(functools.partial(kernel, tp_count, groups, rank_extent),...  38.6 us
    unnamed x1, local copies, waits for them, and re-layouts  0.8 us

profile of v4, /device:TPU:22, one launch (start us, length us, event | category | flops | bytes accessed | tf_op | source)
XLA Modules:
  0.0 39.4 jit_solution(296120905971240325)
XLA Ops:
  0.0 38.6 %query_projection.1 = bf16[128,2048]{1,0:T(8,128)(2,1)S(1)} custom-call(bf16[512,2048]{1,0:T(8,128)(2,1)} %bitcast.5, bf16[2048,2048]{1,0:T(8,128)(2,1)} %weight_hbm.1, bf16[192,2048]{1,0:T(8,128)(2,1)} %bitcast.6, bf16[192,2048]{1,0:T(8,128)(2,1)} %bitcast.7, s32[2,8]{1,0:T(2,128)} %ids_hbm.1, s32[1,8]{1,0:T(1,128)} %lengths_hbm.1, s32[24]{0:T(128)} %slots_hbm.1), custom_call_target="tpu_custom_call" | custom-call | flops 4294967296 | bytes 10485760 | tf_op jit(solution)/shard_map/query_projection/pallas_call | solution.py:530
  38.6 0.8 %copy.9 = bf16[1,128,2048]{2,1,0:T(8,128)(2,1)} copy(bf16[1,128,2048]{2,1,0:T(8,128)(2,1)S(1)} %bitcast.4) | data formatting | bytes 1048576

commit v5 on v4

--- a/solution.py
+++ b/solution.py
@@ -362,8 +362,7 @@
 
         k_right = s - LAG * z
 
-        @pl.when((k_right >= DEPTH) & (k_right < right_count + DEPTH))
-        def _():
+        def right_sent():
             @pl.when((z == 0) & (k_right == DEPTH))
             def _():
                 for i in range(len(PIECES)):
@@ -372,6 +371,10 @@
             @pl.when((z != 0) | (k_right > DEPTH))
             def _():
                 right_copy(k_right - DEPTH).wait_send()
+
+        @pl.when((k_right >= DEPTH) & (k_right >= right_count) & (k_right < right_count + DEPTH))
+        def _():
+            right_sent()
 
         @pl.when((k_right >= 0) & (k_right < right_count))
         def _():
@@ -398,14 +401,17 @@
 
                 stage[at] = (part.astype(F32) + from_left[k_right].astype(F32)).astype(BF16)
 
+            @pl.when(k_right >= DEPTH)
+            def _():
+                right_sent()
+
             @pl.when((z != 0) | (s > 0))
             def _():
                 right_copy(k_right).start()
 
         k_left = s - LAG * (last - z)
 
-        @pl.when((k_left >= DEPTH) & (k_left < left_count + DEPTH))
-        def _():
+        def left_sent():
             @pl.when((z == last) & (k_left == DEPTH))
             def _():
                 for i in range(len(PIECES)):
@@ -414,6 +420,10 @@
             @pl.when((z != last) | (k_left > DEPTH))
             def _():
                 left_copy(k_left - DEPTH).wait_send()
+
+        @pl.when((k_left >= DEPTH) & (k_left >= left_count) & (k_left < left_count + DEPTH))
+        def _():
+            left_sent()
 
         @pl.when((k_left >= 0) & (k_left < left_count))
         def _():
@@ -438,6 +448,10 @@
                     left_copy(k_left).wait_recv()
 
                 stage[k_left] = (part.astype(F32) + from_right[k_left].astype(F32)).astype(BF16)
+
+            @pl.when(k_left >= DEPTH)
+            def _():
+                left_sent()
 
             @pl.when((z != last) | (s > 0))
             def _():

time: 39.5 us -> 39.5 us (level)
  no operation moved by 1% of the time
where the time goes in v5:
time: 39.5 us; the launch traced here: 39.4 us
  Pallas kernels  38.6 us (98%)
  local copies, waits for them, and re-layouts  0.8 us (2%)
    pallas_call x1, Pallas kernels, local(): pl.pallas_call(functools.partial(kernel, tp_count, groups, rank_extent),...  38.6 us
    unnamed x1, local copies, waits for them, and re-layouts  0.8 us

profile of v5, /device:TPU:22, one launch (start us, length us, event | category | flops | bytes accessed | tf_op | source)
XLA Modules:
  0.0 39.4 jit_solution(15415845614358541567)
XLA Ops:
  0.0 38.6 %query_projection.1 = bf16[128,2048]{1,0:T(8,128)(2,1)S(1)} custom-call(bf16[512,2048]{1,0:T(8,128)(2,1)} %bitcast.5, bf16[2048,2048]{1,0:T(8,128)(2,1)} %weight_hbm.1, bf16[192,2048]{1,0:T(8,128)(2,1)} %bitcast.6, bf16[192,2048]{1,0:T(8,128)(2,1)} %bitcast.7, s32[2,8]{1,0:T(2,128)} %ids_hbm.1, s32[1,8]{1,0:T(1,128)} %lengths_hbm.1, s32[24]{0:T(128)} %slots_hbm.1), custom_call_target="tpu_custom_call" | custom-call | flops 4294967296 | bytes 10485760 | tf_op jit(solution)/shard_map/query_projection/pallas_call | solution.py:544
  38.6 0.8 %copy.9 = bf16[1,128,2048]{2,1,0:T(8,128)(2,1)} copy(bf16[1,128,2048]{2,1,0:T(8,128)(2,1)S(1)} %bitcast.4) | data formatting | bytes 1048576

commit v6 on v5

--- a/solution.py
+++ b/solution.py
@@ -13,7 +13,7 @@
 BLOCK_COLS = 512
 PIECES = ((0, 128), (128, 128), (256, 256))
 LAG = 3
-DEPTH = 2
+DEPTH = 3
 
 MESH = pl.DeviceIdType.MESH
 F32 = jnp.float32

time: 39.5 us -> 39.5 us (level)
  no operation moved by 1% of the time
where the time goes in v6:
time: 39.5 us; the launch traced here: 39.4 us
  Pallas kernels  38.6 us (98%)
  local copies, waits for them, and re-layouts  0.8 us (2%)
    pallas_call x1, Pallas kernels, local(): pl.pallas_call(functools.partial(kernel, tp_count, groups, rank_extent),...  38.6 us
    unnamed x1, local copies, waits for them, and re-layouts  0.8 us

profile of v6, /device:TPU:22, one launch (start us, length us, event | category | flops | bytes accessed | tf_op | source)
XLA Modules:
  0.0 39.4 jit_solution(6878616105452576341)
XLA Ops:
  0.0 38.6 %query_projection.1 = bf16[128,2048]{1,0:T(8,128)(2,1)S(1)} custom-call(bf16[512,2048]{1,0:T(8,128)(2,1)} %bitcast.5, bf16[2048,2048]{1,0:T(8,128)(2,1)} %weight_hbm.1, bf16[192,2048]{1,0:T(8,128)(2,1)} %bitcast.6, bf16[192,2048]{1,0:T(8,128)(2,1)} %bitcast.7, s32[2,8]{1,0:T(2,128)} %ids_hbm.1, s32[1,8]{1,0:T(1,128)} %lengths_hbm.1, s32[24]{0:T(128)} %slots_hbm.1), custom_call_target="tpu_custom_call" | custom-call | flops 4294967296 | bytes 10485760 | tf_op jit(solution)/shard_map/query_projection/pallas_call | solution.py:544
  38.6 0.8 %copy.9 = bf16[1,128,2048]{2,1,0:T(8,128)(2,1)} copy(bf16[1,128,2048]{2,1,0:T(8,128)(2,1)S(1)} %bitcast.4) | data formatting | bytes 1048576
